TPU v7x, 128 devices: a whole 4x4x4 slice. The times are simulated.
128 devices in a mesh: row: 8 (over z_lo, y), col: 16 (over z_hi, x, core).
Axes of the slice: x: 4, y: 4, z: 4 (z_hi: 2, z_lo: 2; z = z_hi * 2 + z_lo), core: 2. Of those that a mesh axis runs over, the one named last changes fastest.
Arguments:
- records: bfloat16 [2048, 19200], P(None, ('row', 'col')), may hold values from -40 to 40
- assignment: int32 [2048], replicated, may hold values from 0 to 2047, each once
- channel_flags: int32 [32, 2048], replicated, may hold values from 0 to 1, as said below
Outputs:
- correlations: bfloat16 [2048, 2048, 256], P('row', 'col')
Inputs may be any that keep to these rules, and one draw needn't show every extreme that they name: `channel_flags`: exactly 16 channels are bad in every window.
All inputs are finite; a program needn't handle non-finite values.
Results may differ from a plain program's by a relative error of at most 0.0066.
Values may be sent and summed in bfloat16 or wider, within the bound.
No kernel may reach another device: no remote copies, remote signals or barrier semaphores. Data moves between devices by JAX's collectives and lax.ppermute only.
A program may use at most 192 MiB of HBM per device.

v0:
```python
import math

import jax
import jax.numpy as jnp
from jax import lax
from jax.sharding import PartitionSpec as P

SAMPLES = 600
NFFT = 1024
FIRST_BIN = 10
BINS = 256
MAX_LAG = 128
SMOOTH_HALF = 4
WINDOWS = 32


water_frac = 0.1


def forward_table():
    sample_idx = jnp.arange(SAMPLES, dtype=jnp.int32)
    band_bins = FIRST_BIN + jnp.arange(BINS, dtype=jnp.int32)
    phase = sample_idx[:, None] * band_bins[None, :] % NFFT
    angle = 2.0 * math.pi / NFFT * phase.astype(jnp.float32)
    return jnp.concatenate([jnp.cos(angle), -jnp.sin(angle)], axis=1).astype(jnp.bfloat16)


def inverse_table():
    band_bins = FIRST_BIN + jnp.arange(BINS, dtype=jnp.int32)
    lag_values = jnp.arange(2 * MAX_LAG, dtype=jnp.int32) - MAX_LAG
    phase = band_bins[:, None] * lag_values[None, :] % NFFT
    angle = 2.0 * math.pi / NFFT * phase.astype(jnp.float32)
    return jnp.concatenate([jnp.cos(angle), -jnp.sin(angle)], axis=0).astype(jnp.bfloat16)


def smooth_bins(spectral_power):
    padded = jnp.pad(spectral_power, ((0, 0), (0, 0), (SMOOTH_HALF, SMOOTH_HALF)))
    total = padded[..., 0:BINS]
    for offset in range(1, 2 * SMOOTH_HALF + 1):
        total = total + padded[..., offset : offset + BINS]
    return total / (2 * SMOOTH_HALF + 1)


def whiten(samples, keep_flags):
    shaped = samples.reshape(samples.shape[0], WINDOWS, SAMPLES)
    spectrum = jnp.einsum(
        "nws,sf->nwf", shaped, forward_table(), preferred_element_type=jnp.float32
    )
    real_part = spectrum[..., :BINS]
    imag_part = spectrum[..., BINS:]
    spectral_power = real_part * real_part + imag_part * imag_part
    smoothed = smooth_bins(spectral_power)
    water_level = jnp.mean(spectral_power, axis=-1, keepdims=True)
    inverse_amp = (
        lax.rsqrt(smoothed + water_frac * water_level + 1e-06)
        * jnp.transpose(keep_flags)[:, :, None]
    )
    return (spectrum * jnp.concatenate([inverse_amp, inverse_amp], axis=-1)).astype(jnp.bfloat16)


def make_paired(second_white):
    pair_cols = second_white.shape[0]
    quads = second_white.reshape(pair_cols, WINDOWS, 2, BINS)
    swapped = jnp.stack([-quads[:, :, 1], quads[:, :, 0]], axis=2)
    return jnp.stack([quads, swapped], axis=1).reshape(pair_cols, 2, 2 * WINDOWS, BINS)


def pair_rows(white_rows, paired, pair_scale):
    row_total = white_rows.shape[0]
    pair_cols = paired.shape[0]
    flat_rows = white_rows.reshape(row_total, 2 * WINDOWS, BINS)
    cross_spec = jnp.einsum("pxk,qyxk->pqyk", flat_rows, paired, preferred_element_type=jnp.float32)
    stacked = (cross_spec * pair_scale[:, :, None, None]).astype(jnp.bfloat16)
    stacked = stacked.reshape(row_total * pair_cols, 2 * BINS)
    lagged = jnp.dot(stacked, inverse_table(), preferred_element_type=jnp.float32) * (
        1.0 / math.sqrt(BINS)
    )
    return lagged.astype(jnp.bfloat16).reshape(row_total, pair_cols, 2 * MAX_LAG)


def pair_block(white_rows, paired, pair_scale):
    row_total = white_rows.shape[0]
    blocks_count = row_total // 32
    row_blocks = white_rows.reshape(blocks_count, 32, WINDOWS, 2 * BINS)
    scale_blocks = pair_scale.reshape(blocks_count, 32, pair_scale.shape[1])
    result = lax.map(
        lambda member_pair: pair_rows(member_pair[0], paired, member_pair[1]),
        (row_blocks, scale_blocks),
    )
    return result.reshape(row_total, paired.shape[0], 2 * MAX_LAG)


def per_device(records, assignment, channel_flags):
    row_count = lax.axis_size("row")
    col_count = lax.axis_size("col")
    channel_total = assignment.shape[0]
    group_size = channel_total // (row_count * col_count)
    row_index = lax.axis_index("row")
    col_index = lax.axis_index("col")
    layout = assignment.reshape(row_count, col_count, group_size)
    row_chans = lax.dynamic_index_in_dim(layout, row_index, 0, keepdims=False).reshape(-1)
    col_chans = lax.dynamic_index_in_dim(layout, col_index, 1, keepdims=False).reshape(-1)
    own_row = lax.dynamic_index_in_dim(layout, row_index, 0, keepdims=False)
    own_chans = lax.dynamic_index_in_dim(own_row, col_index, 0, keepdims=False)
    flags = channel_flags.astype(jnp.float32)
    row_flags = jnp.take(flags, row_chans, axis=1)
    col_flags = jnp.take(flags, col_chans, axis=1)
    own_flags = jnp.take(flags, own_chans, axis=1)
    shared = jnp.dot(jnp.transpose(row_flags), col_flags, precision=lax.Precision.HIGHEST)
    pair_scale = lax.rsqrt(jnp.maximum(shared, 1.0))
    ordered = jnp.take(records, assignment, axis=0)
    grouped = lax.all_to_all(ordered, ("row", "col"), split_axis=0, concat_axis=1, tiled=True)
    own_white = whiten(grouped, own_flags)
    col_white = lax.all_gather(own_white, "row", axis=0, tiled=True)
    paired = make_paired(col_white)
    return pair_block(lax.all_gather(own_white, "col", axis=0, tiled=True), paired, pair_scale)


def solution(mesh):
    placed = (P(None, ("row", "col")), P(), P())
    return jax.shard_map(
        per_device, mesh=mesh, in_specs=placed, out_specs=P("row", "col", None), check_vma=False
    )
```

profile of v0, /device:TPU:1, one launch (start us, length us, event | category | flops | bytes accessed | tf_op | source)
XLA Modules:
  0.0 325.5 jit_solution(7902426711940335079)
XLA Ops:
  9.4 7.5 %gather_fusion = bf16[2048,150]{1,0:T(8,128)(2,1)S(1)} fusion(bf16[2048,150]{1,0:T(8,128)(2,1)S(1)} %copy.19, s32[2048]{0:T(1024)S(1)} %fusion.42), kind=kCustom, calls=%fused_computation | custom fusion | bytes 1236992 | tf_op jit(solution)/shard_map/jit(_take)/gather | solution.py:111
  18.2 11.5 %all-to-all-start = ((bf16[128,16,150]{2,1,0:T(8,128)(2,1)}), bf16[128,16,150]{2,1,0:T(8,128)(2,1)S(1)}, u32[]{:S(2)}, u32[]{:S(2)}) async-start(bf16[128,16,150]{2,1,0:T(8,128)(2,1)} %broadcast_select_fusion), calls=%async_computation | async-start | bytes 2097152 | tf_op jit(solution)/shard_map/all_to_all | solution.py:112
  34.1 14.7 %all-to-all-done = bf16[128,16,150]{2,1,0:T(8,128)(2,1)S(1)} async-done(((bf16[128,16,150]{2,1,0:T(8,128)(2,1)}), bf16[128,16,150]{2,1,0:T(8,128)(2,1)S(1)}, u32[]{:S(2)}, u32[]{:S(2)}) %all-to-all-start) | async-done | bytes 614432 | tf_op jit(solution)/shard_map/all_to_all | solution.py:112
  58.9 44.8 %all-gather.5.cloned.1.call-done = bf16[128,32,512]{2,1,0:T(8,128)(2,1)} async-done(((bf16[16,32,512]{2,1,0:T(8,128)(2,1)}), bf16[128,32,512]{2,1,0:T(8,128)(2,1)}) %all-gather.5.cloned.1.call-update) | async-done | bytes 4194320 | tf_op jit(solution)/shard_map/all_gather | solution.py:114
  103.7 6.9 %reshape.191 = bf16[128,32,2,256]{3,2,1,0:T(2,128)(2,1)} reshape(bf16[128,32,512]{2,1,0:T(8,128)(2,1)} %all-gather.5.cloned.1.call-done) | data formatting | bytes 8388608 | tf_op jit(solution)/shard_map/reshape | solution.py:63
  110.7 10.9 %slice_negate_fusion = (bf16[128,32,1,256]{3,2,1,0:T(2,128)(2,1)S(1)}, bf16[128,32,1,256]{3,2,1,0:T(2,128)(2,1)S(1)}) fusion(bf16[128,32,2,256]{3,2,1,0:T(2,128)(2,1)} %reshape.191), kind=kLoop, calls=%fused_computation.30 | loop fusion | flops 1048576 | bytes 8388608 | tf_op jit(solution)/shard_map/neg | solution.py:64
  121.6 10.5 %pad_maximum_fusion.1 = bf16[128,32,2,256]{3,2,1,0:T(2,128)(2,1)} fusion(bf16[128,32,1,256]{3,2,1,0:T(2,128)(2,1)S(1)} %get-tuple-element.92, bf16[128,32,1,256]{3,2,1,0:T(2,128)(2,1)S(1)} %get-tuple-element.91), kind=kLoop, calls=%fused_computation.31 | loop fusion | flops 8388608 | bytes 8388608 | tf_op jit(solution)/shard_map/stack | solution.py:64
  132.1 15.2 %copy.22 = bf16[128,32,2,256]{0,2,1,3:T(2,128)(2,1)} copy(bf16[128,32,2,256]{3,2,1,0:T(2,128)(2,1)} %pad_maximum_fusion.1) | data formatting | bytes 8388608 | tf_op jit(solution)/shard_map/stack | solution.py:64
  147.4 7.1 %stack.12 = bf16[128,1,64,256]{3,2,0,1:T(8,128)(2,1)} reshape(bf16[128,32,512]{2,1,0:T(8,128)(2,1)} %all-gather.5.cloned.1.call-done) | data formatting | bytes 8388608 | tf_op jit(solution)/shard_map/stack | solution.py:65
  154.5 7.4 %copy.23 = bf16[128,1,64,256]{0,2,1,3:T(8,128)(2,1)} copy(bf16[128,1,64,256]{3,2,0,1:T(8,128)(2,1)} %stack.12) | data formatting | bytes 8388608 | tf_op jit(solution)/shard_map/stack | solution.py:65
  161.9 7.5 %pad_maximum_fusion = bf16[128,2,64,256]{0,2,1,3:T(8,128)(2,1)} fusion(bf16[128,1,64,256]{0,2,1,3:T(8,128)(2,1)} %bitcast.56, bf16[128,1,64,256]{0,2,1,3:T(8,128)(2,1)} %copy.23), kind=kLoop, calls=%fused_computation.29 | loop fusion | flops 4194304 | bytes 16777216 | tf_op jit(solution)/shard_map/stack | solution.py:65
  169.4 8.7 %all-gather.3.cloned.1.call-done = bf16[256,32,512]{2,1,0:T(8,128)(2,1)} async-done(((bf16[16,32,512]{2,1,0:T(8,128)(2,1)}), bf16[256,32,512]{2,1,0:T(8,128)(2,1)}) %all-gather.3.cloned.1.call-update) | async-done | bytes 8388624 | tf_op jit(solution)/shard_map/all_gather | solution.py:116
  178.1 140.6 %while.12 = (s32[]{:T(128)}, bf16[8,32,128,256]{3,2,1,0:T(8,128)(2,1)}, bf16[8,32,32,512]{3,2,1,0:T(8,128)(2,1)}, bf16[128,2,64,256]{0,2,1,3:T(8,128)(2,1)}, f32[8,32,128]{2,1,0:T(8,128)S(1)}, /*index=5*/s32[]{:T(128)}) while((s32[]{:T(128)}, bf16[8,32,128,256]{3,2,1,0:T(8,128)(2,1)}, bf16[8,32,32,512]{3,2,1,0:T(8,128)(2,1)}, ...), condition=%wide.region_2.3_spmd, body=%wide.region_1.2_spmd.sunk | while | flops 1350107648 | bytes 39375436 | solution.py:86
  182.9 4.7 %fusion.63 = bf16[32,128,2,256]{1,0,2,3:T(8,128)(2,1)S(1)} fusion(f32[32,128]{1,0:T(8,128)S(1)} %dynamic-slice_bitcast_fusion.2, bf16[32,64,256,1]{1,0,3,2:T(8,128)(2,1)S(1)} %copy.36, bf16[128,2,64,256]{0,2,1,3:T(8,128)(2,1)} %get-tuple-element.151), kind=kOutput, calls=%fused_computation.7.clone.1 | convolution fusion | flops 272629760 | bytes 13647872 | tf_op jit(solution)/shard_map/while/body/eval_jaxpr/pxk,qyxk->pqyk/dot_general | solution.py:72
  200.4 4.7 %fusion.63 = bf16[32,128,2,256]{1,0,2,3:T(8,128)(2,1)S(1)} fusion(f32[32,128]{1,0:T(8,128)S(1)} %dynamic-slice_bitcast_fusion.2, bf16[32,64,256,1]{1,0,3,2:T(8,128)(2,1)S(1)} %copy.36, bf16[128,2,64,256]{0,2,1,3:T(8,128)(2,1)} %get-tuple-element.151), kind=kOutput, calls=%fused_computation.7.clone.1 | convolution fusion | flops 272629760 | bytes 13647872 | tf_op jit(solution)/shard_map/while/body/eval_jaxpr/pxk,qyxk->pqyk/dot_general | solution.py:72
  218.0 4.7 %fusion.63 = bf16[32,128,2,256]{1,0,2,3:T(8,128)(2,1)S(1)} fusion(f32[32,128]{1,0:T(8,128)S(1)} %dynamic-slice_bitcast_fusion.2, bf16[32,64,256,1]{1,0,3,2:T(8,128)(2,1)S(1)} %copy.36, bf16[128,2,64,256]{0,2,1,3:T(8,128)(2,1)} %get-tuple-element.151), kind=kOutput, calls=%fused_computation.7.clone.1 | convolution fusion | flops 272629760 | bytes 13647872 | tf_op jit(solution)/shard_map/while/body/eval_jaxpr/pxk,qyxk->pqyk/dot_general | solution.py:72
  224.8 4.4 %fusion.64 = bf16[4096,256]{1,0:T(8,128)(2,1)S(1)} fusion(bf16[64,8,32,128]{3,2,1,0:T(8,128)(2,1)S(1)} %bitcast.54, bf16[256,256]{1,0:T(8,128)(2,1)S(1)} %get-tuple-element.134, bf16[256,256]{1,0:T(8,128)(2,1)S(1)} %get-tuple-element.135), kind=kOutput, calls=%fused_computation.6.clone.1 | convolution fusion | flops 1076363264 | bytes 6553600 | tf_op jit(solution)/shard_map/while/body/eval_jaxpr/dot_general | solution.py:75
  235.6 4.7 %fusion.63 = bf16[32,128,2,256]{1,0,2,3:T(8,128)(2,1)S(1)} fusion(f32[32,128]{1,0:T(8,128)S(1)} %dynamic-slice_bitcast_fusion.2, bf16[32,64,256,1]{1,0,3,2:T(8,128)(2,1)S(1)} %copy.36, bf16[128,2,64,256]{0,2,1,3:T(8,128)(2,1)} %get-tuple-element.151), kind=kOutput, calls=%fused_computation.7.clone.1 | convolution fusion | flops 272629760 | bytes 13647872 | tf_op jit(solution)/shard_map/while/body/eval_jaxpr/pxk,qyxk->pqyk/dot_general | solution.py:72
  253.2 4.7 %fusion.63 = bf16[32,128,2,256]{1,0,2,3:T(8,128)(2,1)S(1)} fusion(f32[32,128]{1,0:T(8,128)S(1)} %dynamic-slice_bitcast_fusion.2, bf16[32,64,256,1]{1,0,3,2:T(8,128)(2,1)S(1)} %copy.36, bf16[128,2,64,256]{0,2,1,3:T(8,128)(2,1)} %get-tuple-element.151), kind=kOutput, calls=%fused_computation.7.clone.1 | convolution fusion | flops 272629760 | bytes 13647872 | tf_op jit(solution)/shard_map/while/body/eval_jaxpr/pxk,qyxk->pqyk/dot_general | solution.py:72
  260.0 4.4 %fusion.64 = bf16[4096,256]{1,0:T(8,128)(2,1)S(1)} fusion(bf16[64,8,32,128]{3,2,1,0:T(8,128)(2,1)S(1)} %bitcast.54, bf16[256,256]{1,0:T(8,128)(2,1)S(1)} %get-tuple-element.134, bf16[256,256]{1,0:T(8,128)(2,1)S(1)} %get-tuple-element.135), kind=kOutput, calls=%fused_computation.6.clone.1 | convolution fusion | flops 1076363264 | bytes 6553600 | tf_op jit(solution)/shard_map/while/body/eval_jaxpr/dot_general | solution.py:75
  270.8 4.7 %fusion.63 = bf16[32,128,2,256]{1,0,2,3:T(8,128)(2,1)S(1)} fusion(f32[32,128]{1,0:T(8,128)S(1)} %dynamic-slice_bitcast_fusion.2, bf16[32,64,256,1]{1,0,3,2:T(8,128)(2,1)S(1)} %copy.36, bf16[128,2,64,256]{0,2,1,3:T(8,128)(2,1)} %get-tuple-element.151), kind=kOutput, calls=%fused_computation.7.clone.1 | convolution fusion | flops 272629760 | bytes 13647872 | tf_op jit(solution)/shard_map/while/body/eval_jaxpr/pxk,qyxk->pqyk/dot_general | solution.py:72
  288.3 4.7 %fusion.63 = bf16[32,128,2,256]{1,0,2,3:T(8,128)(2,1)S(1)} fusion(f32[32,128]{1,0:T(8,128)S(1)} %dynamic-slice_bitcast_fusion.2, bf16[32,64,256,1]{1,0,3,2:T(8,128)(2,1)S(1)} %copy.36, bf16[128,2,64,256]{0,2,1,3:T(8,128)(2,1)} %get-tuple-element.151), kind=kOutput, calls=%fused_computation.7.clone.1 | convolution fusion | flops 272629760 | bytes 13647872 | tf_op jit(solution)/shard_map/while/body/eval_jaxpr/pxk,qyxk->pqyk/dot_general | solution.py:72
  295.1 4.4 %fusion.64 = bf16[4096,256]{1,0:T(8,128)(2,1)S(1)} fusion(bf16[64,8,32,128]{3,2,1,0:T(8,128)(2,1)S(1)} %bitcast.54, bf16[256,256]{1,0:T(8,128)(2,1)S(1)} %get-tuple-element.134, bf16[256,256]{1,0:T(8,128)(2,1)S(1)} %get-tuple-element.135), kind=kOutput, calls=%fused_computation.6.clone.1 | convolution fusion | flops 1076363264 | bytes 6553600 | tf_op jit(solution)/shard_map/while/body/eval_jaxpr/dot_general | solution.py:75
  305.9 4.7 %fusion.63 = bf16[32,128,2,256]{1,0,2,3:T(8,128)(2,1)S(1)} fusion(f32[32,128]{1,0:T(8,128)S(1)} %dynamic-slice_bitcast_fusion.2, bf16[32,64,256,1]{1,0,3,2:T(8,128)(2,1)S(1)} %copy.36, bf16[128,2,64,256]{0,2,1,3:T(8,128)(2,1)} %get-tuple-element.151), kind=kOutput, calls=%fused_computation.7.clone.1 | convolution fusion | flops 272629760 | bytes 13647872 | tf_op jit(solution)/shard_map/while/body/eval_jaxpr/pxk,qyxk->pqyk/dot_general | solution.py:72
  (115 shorter events, 107.5 us)
Async XLA Ops:
  17.0 12.8 %copy-start.1 = (s32[2048]{0:T(1024)S(1)}, s32[2048]{0:T(1024)}, u32[]{:S(2)}) copy-start(s32[2048]{0:T(1024)} %param.6) | copy-start | bytes 24580
  17.0 12.9 %copy-start = (s32[32,2048]{1,0:T(8,128)S(1)}, s32[32,2048]{1,0:T(8,128)}, u32[]{:S(2)}) copy-start(s32[32,2048]{1,0:T(8,128)} %param.7) | copy-start | bytes 786436
  18.2 30.6 %all-to-all-start = ((bf16[128,16,150]{2,1,0:T(8,128)(2,1)}), bf16[128,16,150]{2,1,0:T(8,128)(2,1)S(1)}, u32[]{:S(2)}, u32[]{:S(2)}) async-start(bf16[128,16,150]{2,1,0:T(8,128)(2,1)} %broadcast_select_fusion), calls=%async_computation | async-start | bytes 2097152 | tf_op jit(solution)/shard_map/all_to_all | solution.py:112
  29.7 74.0 %all-gather.5.cloned.1.call-start = ((), (), s32[]{:S(2)}) async-start(), calls=%async_computation.2 | async-start | bytes 4718592 | tf_op jit(solution)/shard_map/all_gather | solution.py:114
  54.8 123.3 %all-gather.3.cloned.1.call-start = ((), (), s32[]{:S(2)}) async-start(), calls=%async_computation.1 | async-start | bytes 8912896 | tf_op jit(solution)/shard_map/all_gather | solution.py:116
Sparse Core Ops, SparseCore 0:
  54.9 48.7 all-gather.4
  106.2 71.8 all-gather.2
where the time goes:
time: 327 us; the launch traced here: 326 us
  local copies, waits for them, and re-layouts  108 us (33%)
  matrix products  75.2 us (23%)
  waiting for transfers between devices  68.7 us (21%)
  other arithmetic  47.6 us (15%)
  between operations  13.6 us (4%)
  starting transfers between devices  11.8 us (4%)
    all_gather x1, waiting for transfers between devices, per_device(): col_white = lax.all_gather(own_white, 'row', axis=0, tiled=True)  44.8 us
    dot_general x8, matrix products, pair_rows(): jnp.einsum('pxk,qyxk->pqyk', flat_rows, paired, preferred_element_type=jn...  37.7 us
    dot_general x8, matrix products, pair_rows(): jnp.dot(stacked, inverse_table(), preferred_element_type=jnp.float32)  35.6 us
    reshape x16, local copies, waits for them, and re-layouts, pair_rows(): flat_rows = white_rows.reshape(row_total, 2 * WINDOWS, BINS)  27.7 us
    another operation x1, local copies, waits for them, and re-layouts, make_paired(): swapped = jnp.stack([-quads[:, :, 1], quads[:, :, 0]], axis=2)  15.2 us
    all_to_all x1, waiting for transfers between devices, per_device(): lax.all_to_all(ordered, ('row', 'col'), split_axis=0, concat_axis=1, tile...  14.7 us
    another operation x2, local copies, waits for them, and re-layouts, make_paired(): jnp.stack([quads, swapped], axis=1).reshape(pair_cols, 2, 2 * WINDOWS, BINS)  14.6 us
    another operation x9, other arithmetic  13.3 us
  transfers between devices with their start and end apart: 3, of which 3 were waited for; matrix products, arithmetic and copies ran while one was open for 22% of the time, Pallas kernels for 0%

commit v1 on v0

v1 whole, which is shorter than its diff:
```python
import math

import jax
import jax.numpy as jnp
import numpy as np
from jax import lax
from jax.experimental import pallas as pl
from jax.experimental.pallas import tpu as pltpu
from jax.sharding import PartitionSpec as P

SAMPLES = 600
NFFT = 1024
FIRST_BIN = 10
BINS = 256
MAX_LAG = 128
WINDOWS = 32
CHANS = 2048
GROUP = 16
SLICE = 150
QUARTERS = 4
KGS = 64
PITCH = 264

f32 = jnp.float32
bf16 = jnp.bfloat16
vmem = pl.BlockSpec(memory_space=pltpu.VMEM)
smem = pl.BlockSpec(memory_space=pltpu.SMEM)
anym = pl.BlockSpec(memory_space=pl.ANY)


def forward_table():
    phase = (FIRST_BIN + np.arange(BINS))[None, :] * np.arange(SAMPLES)[:, None] % NFFT
    angle = 2.0 * math.pi / NFFT * phase
    table = np.concatenate([np.cos(angle), -np.sin(angle)], axis=1)
    return jnp.asarray(table.reshape(QUARTERS, SLICE, 2 * BINS), bf16)


def lag_table():
    phase = (FIRST_BIN + np.arange(BINS))[None, :] * (np.arange(2 * MAX_LAG) - MAX_LAG)[:, None] % NFFT
    angle = 2.0 * math.pi / NFFT * phase
    table = np.concatenate([np.cos(angle), -np.sin(angle)], axis=1)
    return jnp.asarray(jnp.asarray(table, bf16).astype(f32) / math.sqrt(BINS), bf16)


def order_channels(records_t, assignment):
    block = 512

    def kernel(assign_ref, rec_ref, out_ref, turn_ref):
        chan = lax.broadcasted_iota(jnp.int32, (CHANS, block), 0)
        onehot = (chan == assign_ref[...]).astype(f32).astype(bf16)
        turn_ref[0:SLICE, :] = jnp.dot(rec_ref[...], onehot, preferred_element_type=f32)
        out_ref[...] = turn_ref[...].T[:, :SLICE].astype(bf16)

    return pl.pallas_call(
        kernel,
        out_shape=jax.ShapeDtypeStruct((CHANS, SLICE), bf16),
        grid=(CHANS // block,),
        in_specs=[
            pl.BlockSpec((1, block), lambda i: (0, i)),
            pl.BlockSpec((SLICE, CHANS), lambda i: (0, 0)),
        ],
        out_specs=pl.BlockSpec((block, SLICE), lambda i: (i, 0)),
        scratch_shapes=[pltpu.VMEM((256, block), f32)],
        compiler_params=pltpu.CompilerParams(vmem_limit_bytes=40 * 2**20),
    )(assignment.reshape(1, CHANS), records_t)


def whiten(slices, keep, table):
    def kernel(x_ref, keep_ref, f_ref, out_ref, z0, z1, z2, z3, turn_ref):
        zs = [z0, z1, z2, z3]
        spec = None
        for quarter in range(QUARTERS):
            rows = jnp.concatenate([x_ref[QUARTERS * w + quarter] for w in range(WINDOWS)], axis=0)
            part = jnp.dot(rows, f_ref[quarter], preferred_element_type=f32)
            spec = part if spec is None else spec + part
        re, im = spec[:, :BINS], spec[:, BINS:]
        power = re * re + im * im
        water = jnp.mean(power, axis=1, keepdims=True)
        padded = jnp.concatenate([power, jnp.zeros((512, 128), f32)], axis=1)
        total = padded + pltpu.roll(padded, 1, 1)
        total = total + pltpu.roll(total, 2, 1)
        total = total + pltpu.roll(total, 4, 1)
        total = total + pltpu.roll(padded, 8, 1)
        smooth = pltpu.roll(total, 384 - 4, 1)[:, :BINS]
        amp = lax.rsqrt(smooth / 9.0 + 0.1 * water + 1e-6) * keep_ref[...]
        for h in range(4):
            zs[h][...] = spec[:, h * 128 : (h + 1) * 128] * amp[:, (h % 2) * 128 : (h % 2) * 128 + 128]
        low = lax.broadcasted_iota(jnp.int32, (WINDOWS, 128), 1) < 64
        for ri in range(2):
            for pair in range(GROUP // 2):
                rows = []
                for h in range(2):
                    first = zs[2 * ri + h][pl.ds(2 * pair, WINDOWS, stride=GROUP), :]
                    second = zs[2 * ri + h][pl.ds(2 * pair + 1, WINDOWS, stride=GROUP), :]
                    rows.append(jnp.where(low, first, pltpu.roll(second, 64, 1)))
                    rows.append(jnp.where(low, pltpu.roll(first, 64, 1), second))
                turned = jnp.concatenate(rows, axis=0).T
                for j in range(2):
                    turn_ref[pl.ds(ri * GROUP + 2 * pair + j, KGS, stride=2 * GROUP), :] = turned[
                        j * KGS : (j + 1) * KGS
                    ]
        out_ref[...] = turn_ref[...].astype(bf16)

    out = pl.pallas_call(
        kernel,
        out_shape=jax.ShapeDtypeStruct((KGS * 2 * GROUP, 128), bf16),
        in_specs=[vmem] * 3,
        out_specs=vmem,
        scratch_shapes=[pltpu.VMEM((512, 128), f32)] * 4 + [pltpu.VMEM((KGS * 2 * GROUP, 128), f32)],
        compiler_params=pltpu.CompilerParams(vmem_limit_bytes=40 * 2**20),
    )(slices, keep, table)
    return out.reshape(KGS, 2, GROUP, 128)


def turn_second(blocks, places):
    flat, kinds = flatten(blocks)

    def kernel(*refs):
        place_ref, out_ref, hold = refs[0], refs[-2], refs[-1]
        for half, parts in enumerate(halves(refs[1:-2], kinds)):

            @pl.loop(0, KGS // 2, unroll=4)
            def _(i):
                kg = half * (KGS // 2) + i
                for ri in range(2):
                    for b, (ref, off) in enumerate(parts):
                        row = pl.multiple_of(place_ref[b] * GROUP, GROUP)
                        hold[kg, ri, pl.ds(row, GROUP), :] = ref[i + off, ri]
                for ri in range(2):
                    out_ref[kg, ri] = hold[kg, ri].T

    return pl.pallas_call(
        kernel,
        out_shape=jax.ShapeDtypeStruct((KGS, 2, 128, 128), bf16),
        in_specs=[smem] + [vmem] * len(flat),
        out_specs=vmem,
        scratch_shapes=[pltpu.VMEM((KGS, 2, 128, 128), bf16)],
        compiler_params=pltpu.CompilerParams(vmem_limit_bytes=40 * 2**20),
        cost_estimate=pl.CostEstimate(flops=4 * 10**9, bytes_accessed=8 * 2**20, transcendentals=0),
    )(places, *flat)


def flatten(blocks):
    flat, kinds = [], []
    for block in blocks:
        kinds.append(len(block))
        flat.extend(block)
    return flat, kinds


def halves(refs, kinds):
    out = [[], []]
    at = 0
    for kind in kinds:
        for half in range(2):
            if kind == 1:
                out[half].append((refs[at], half * (KGS // 2)))
            else:
                out[half].append((refs[at + half], 0))
        at += kind
    return out


def pair_chunk(blocks, places, second, scale, table, result):
    flat, kinds = flatten(blocks)
    count = len(blocks)
    rows = count * GROUP

    def kernel(*refs):
        place_ref, sec_ref, scale_ref, tab_ref = refs[:4]
        firsts = refs[4 : 4 + len(flat)]
        out_hbm, spec_re, spec_im, stage, sems = refs[-5:]
        lane = lax.broadcasted_iota(jnp.int32, (rows, 256), 1) % 128 // 32
        starts = [pl.multiple_of(place_ref[b] * GROUP, GROUP) for b in range(count)]
        scales = jnp.concatenate([scale_ref[pl.ds(s, GROUP), :] for s in starts], axis=0)
        for half, parts in enumerate(halves(firsts, kinds)):

            @pl.loop(0, KGS // 2, unroll=8)
            def _(i):
                kg = half * (KGS // 2) + i
                vr, vi = sec_ref[kg, 0], sec_ref[kg, 1]
                rhs = jnp.concatenate(
                    [jnp.concatenate([vr, -vi], axis=1), jnp.concatenate([vi, vr], axis=1)], axis=0
                )
                lhs = jnp.concatenate(
                    [jnp.concatenate([ref[i + off, ri] for ref, off in parts], axis=0) for ri in range(2)],
                    axis=1,
                )
                lhs = jnp.concatenate(
                    [jnp.where(lane == ki, lhs, jnp.zeros_like(lhs)) for ki in range(4)], axis=0
                )
                cross = jnp.dot(lhs, rhs, preferred_element_type=f32)
                for ki in range(4):
                    part = cross[ki * rows : (ki + 1) * rows]
                    spec_re[pl.ds(ki * KGS + kg, rows, stride=PITCH), :] = part[:, :128] * scales
                    spec_im[pl.ds(ki * KGS + kg, rows, stride=PITCH), :] = part[:, 128:] * scales

        def copy_out(b):
            return pltpu.make_async_copy(
                stage.at[pl.ds(b * GROUP, GROUP)], out_hbm.at[pl.ds(starts[b], GROUP)], sems.at[b]
            )

        for b in range(count):

            @pl.loop(0, GROUP // 2, unroll=8)
            def _(i):
                weights = []
                for j in range(2):
                    at = pl.multiple_of((b * GROUP + 2 * i + j) * PITCH, 8)
                    weights.append(
                        jnp.concatenate(
                            [
                                spec_re[pl.ds(at, BINS), :].astype(bf16),
                                spec_im[pl.ds(at, BINS), :].astype(bf16),
                            ],
                            axis=0,
                        )
                    )
                lagged = jnp.dot(
                    tab_ref[...], jnp.concatenate(weights, axis=1), preferred_element_type=f32
                ).astype(bf16)
                for j in range(2):
                    stage[b * GROUP + 2 * i + j] = lagged[:, j * 128 : (j + 1) * 128].T

            copy_out(b).start()
        for b in range(count):
            copy_out(b).wait()

    ins = [places, second, scale, table, *flat]
    specs = [smem, vmem, vmem, vmem] + [vmem] * len(flat)
    aliases = {}
    if result is not None:
        aliases = {len(ins): 0}
        ins.append(result)
        specs.append(anym)
    return pl.pallas_call(
        kernel,
        out_shape=jax.ShapeDtypeStruct((256, 128, 2 * MAX_LAG), bf16),
        in_specs=specs,
        out_specs=anym,
        scratch_shapes=[
            pltpu.VMEM((rows * PITCH, 128), f32),
            pltpu.VMEM((rows * PITCH, 128), f32),
            pltpu.VMEM((rows, 128, 2 * MAX_LAG), bf16),
            pltpu.SemaphoreType.DMA((count,)),
        ],
        input_output_aliases=aliases,
        compiler_params=pltpu.CompilerParams(vmem_limit_bytes=48 * 2**20),
        cost_estimate=pl.CostEstimate(flops=15 * 10**9, bytes_accessed=10 * 2**20, transcendentals=0),
    )(*ins)


def col_perm(dz, dx, dcore):
    def to(i):
        z, x, core = i // 8, i // 2 % 4, i % 2
        return ((z ^ dz) * 4 + (x + dx) % 4) * 2 + (core ^ dcore)

    return [(i, to(i)) for i in range(16)]


def row_perm(dz, dy):
    return [(i, (i // 4 ^ dz) * 4 + (i % 4 + dy) % 4) for i in range(8)]


def ring_of_four(own, axis, up, down):
    below = lax.ppermute(own, axis, up)
    above = lax.ppermute(own, axis, down)
    half = KGS // 2
    far = [lax.ppermute(below[:half], axis, up), lax.ppermute(above[half:], axis, down)]
    return [own], [below], [above], far


def per_device(records, assignment, channel_flags):
    row = lax.axis_index("row")
    col = lax.axis_index("col")
    layout = assignment.reshape(8, 16, GROUP)
    row_chans = lax.dynamic_index_in_dim(layout, row, 0, keepdims=False).reshape(-1)
    col_chans = lax.dynamic_index_in_dim(layout, col, 1, keepdims=False).reshape(-1)
    own_row = lax.dynamic_index_in_dim(layout, row, 0, keepdims=False)
    own_chans = lax.dynamic_index_in_dim(own_row, col, 0, keepdims=False)

    ordered = order_channels(records.T, assignment)
    slices = lax.all_to_all(
        ordered.reshape(128, GROUP, SLICE), ("row", "col"), split_axis=0, concat_axis=0, tiled=True
    )

    flags = channel_flags.astype(f32)
    row_flags = jnp.take(flags, row_chans, axis=1, mode="clip")
    col_flags = jnp.take(flags, col_chans, axis=1, mode="clip")
    keep = jnp.take(flags, own_chans, axis=1, mode="clip").reshape(WINDOWS * GROUP, 1)
    shared = jnp.dot(jnp.transpose(row_flags), col_flags, precision=lax.Precision.HIGHEST)
    scale = lax.rsqrt(jnp.maximum(shared, 1.0))

    own = whiten(slices, keep, forward_table())

    own_zh = lax.ppermute(own, "col", col_perm(1, 0, 0))
    own_zl = lax.ppermute(own, "row", row_perm(1, 0))
    up_y, down_y = row_perm(0, 1), row_perm(0, -1)
    up_x, down_x = col_perm(0, 1, 0), col_perm(0, -1, 0)
    second = ring_of_four(own, "row", up_y, down_y) + ring_of_four(own_zl, "row", up_y, down_y)
    first = ring_of_four(own, "col", up_x, down_x) + ring_of_four(own_zh, "col", up_x, down_x)
    flip = col_perm(0, 0, 1)
    other = [[lax.ppermute(part, "col", flip) for part in block] for block in first]

    z_lo, y = row // 4, row % 4
    z_hi, x, core = col // 8, col // 2 % 4, col % 2
    steps = (0, -1, 1, 2)
    second_places = jnp.stack([(z_lo ^ dz) * 4 + (y + d) % 4 for dz in range(2) for d in steps])
    turned = turn_second(second, second_places.astype(jnp.int32))
    places = [((z_hi ^ dz) * 4 + (x + d) % 4) * 2 for dz in range(2) for d in steps]

    table = lag_table()
    result = None
    for c in range(4):
        members = (2 * c, 2 * c + 1)
        blocks, spots = [], []
        for m in members:
            blocks += [first[m], other[m]]
            spots += [places[m] + core, places[m] + (core ^ 1)]
        result = pair_chunk(blocks, jnp.stack(spots).astype(jnp.int32), turned, scale, table, result)
    return result


def solution(mesh):
    placed = (P(None, ("row", "col")), P(), P())
    return jax.shard_map(
        per_device, mesh=mesh, in_specs=placed, out_specs=P("row", "col", None), check_vma=False
    )
```

time: 327 us -> 153 us (0.47)
  local copies, waits for them, and re-layouts: 108 us -> 22.3 us
  matrix products: 75.2 us -> 1.19 us
  Pallas kernels: 0 us -> 52.5 us
  other arithmetic: 47.6 us -> 0.32 us
  waiting for transfers between devices: 68.7 us -> 30.6 us
  starting transfers between devices: 11.8 us -> 45 us
  between operations: 13.6 us -> 0.57 us
    dot_general x17 -> x0, matrix products: 74.9 us -> none  [the longest x8 37.7 us: pair_rows(): jnp.einsum('pxk,qyxk->pqyk', flat_rows, paired, preferred_element_type=jn...]
    all_gather x2 -> x0, waiting for transfers between devices: 53.5 us -> none  [the longest x1 44.8 us: per_device(): col_white = lax.all_gather(own_white, 'row', axis=0, tiled=True)]
    pallas_call x0 -> x7, Pallas kernels: none -> 52.5 us  [the longest x4 41.5 us: pair_chunk(): pl.pallas_call(kernel, out_shape=jax.ShapeDtypeStruct((256, 128, 2 * MAX_...]
    reshape x23 -> x2, local copies, waits for them, and re-layouts: 36.6 us -> 0.94 us  [the longest x1 0.78 us: per_device(): layout = assignment.reshape(8, 16, GROUP)]
    ppermute x0 -> x28, starting transfers between devices: none -> 33.5 us  [the longest x4 10.3 us: ring_of_four(): lax.ppermute(above[half:], axis, down)]
    another operation x11 -> x3, other arithmetic: 31.3 us -> 0.23 us  [per_device(): jnp.stack(spots).astype(jnp.int32)]
    another operation x3 -> x1, local copies, waits for them, and re-layouts: 29.8 us -> 0.08 us  [per_device(): jnp.stack([(z_lo ^ dz) * 4 + (y + d) % 4 for dz in range(2) for d in steps])]
    ppermute x0 -> x28, waiting for transfers between devices: none -> 14.7 us  [the longest x1 7.34 us: per_device(): own_zh = lax.ppermute(own, 'col', col_perm(1, 0, 0))]
  transfers between devices with their start and end apart: 3 -> 29, of which waited for: 3 -> 3; matrix products, arithmetic and copies ran while one was open for 22% -> 11% of each run, Pallas kernels for 0% -> 23%
where the time goes in v1:
time: 153 us; the launch traced here: 152 us
  Pallas kernels  52.5 us (34%)
  starting transfers between devices  45 us (29%)
  waiting for transfers between devices  30.6 us (20%)
  local copies, waits for them, and re-layouts  22.3 us (15%)
    pallas_call x4, Pallas kernels, pair_chunk(): pl.pallas_call(kernel, out_shape=jax.ShapeDtypeStruct((256, 128, 2 * MAX_...  41.5 us
    all_to_all x1, waiting for transfers between devices, per_device(): lax.all_to_all(ordered.reshape(128, GROUP, SLICE), ('row', 'col'), split_...  15.9 us
    all_to_all x1, starting transfers between devices, per_device(): lax.all_to_all(ordered.reshape(128, GROUP, SLICE), ('row', 'col'), split_...  11.5 us
    ppermute x4, starting transfers between devices, ring_of_four(): lax.ppermute(above[half:], axis, down)  10.3 us
    ppermute x10, starting transfers between devices, per_device(): lax.ppermute(part, 'col', flip)  9.93 us
    ppermute x4, starting transfers between devices, ring_of_four(): above = lax.ppermute(own, axis, down)  9.81 us
    unnamed x19, local copies, waits for them, and re-layouts  8.21 us
    ppermute x1, waiting for transfers between devices, per_device(): own_zh = lax.ppermute(own, 'col', col_perm(1, 0, 0))  7.34 us
  transfers between devices with their start and end apart: 29, of which 3 were waited for; matrix products, arithmetic and copies ran while one was open for 11% of the time, Pallas kernels for 23%

profile of v1, /device:TPU:1, one launch (start us, length us, event | category | flops | bytes accessed | tf_op | source)
XLA Modules:
  0.0 152.4 jit_solution(11627634171140301597)
XLA Ops:
  1.8 3.3 %shard_map.55 = bf16[2048,150]{1,0:T(8,128)(2,1)} custom-call(s32[1,2048]{1,0:T(1,128)S(1)} %bitcast.43, bf16[150,2048]{1,0:T(8,128)(2,1)S(1)} %bitcast.33), custom_call_target="tpu_custom_call" | custom-call | tf_op jit(solution)/shard_map/pallas_call | solution.py:54
  5.1 11.5 %all-to-all-start = ((bf16[128,16,150]{2,1,0:T(8,128)(2,1)}), bf16[128,16,150]{2,1,0:T(8,128)(2,1)S(1)}, u32[]{:S(2)}, u32[]{:S(2)}) async-start(bf16[128,16,150]{2,1,0:T(8,128)(2,1)} %bitcast.14), calls=%async_computation | async-start | bytes 2097152 | tf_op jit(solution)/shard_map/all_to_all | solution.py:283
  19.7 15.9 %all-to-all-done.x_ref = bf16[128,16,150]{2,1,0:T(8,128)(2,1)S(1)} async-done(((bf16[128,16,150]{2,1,0:T(8,128)(2,1)}), bf16[128,16,150]{2,1,0:T(8,128)(2,1)S(1)}, u32[]{:S(2)}, u32[]{:S(2)}) %all-to-all-start) | async-done | bytes 614432 | tf_op jit(solution)/shard_map/all_to_all | solution.py:283
  36.7 3.7 %shard_map.56 = bf16[2048,128]{1,0:T(8,128)(2,1)S(1)} custom-call(bf16[128,16,150]{2,1,0:T(8,128)(2,1)S(1)} %all-to-all-done.x_ref, f32[512,1]{1,0:T(8,128)S(1)} %reshape.56.keep_ref, bf16[4,150,512]{2,1,0:T(8,128)(2,1)S(1)} %copy-done.1), custom_call_target="tpu_custom_call" | custom-call | tf_op jit(solution)/shard_map/pallas_call | solution.py:104
  40.9 2.7 %collective-permute-start.1 = (bf16[64,2,16,128]{3,2,1,0:T(8,128)(2,1)S(1)}, bf16[64,2,16,128]{3,2,1,0:T(8,128)(2,1)S(1)}, u32[]{:S(2)}, u32[]{:S(2)}) collective-permute-start(bf16[64,2,16,128]{3,2,1,0:T(8,128)(2,1)S(1)} %bitcast.36), channel_id=1, source_target_pairs={{0,48},{16,0},{32,16},{48,32},{64,112},{80,64},{96,80},{112,96},{1... | collective-permute-start | bytes 1572872 | tf_op jit(solution)/shard_map/ppermute | solution.py:267
  45.5 7.3 %collective-permute-done.4.refs_6_ = bf16[64,2,16,128]{3,2,1,0:T(8,128)(2,1)} collective-permute-done((bf16[64,2,16,128]{3,2,1,0:T(8,128)(2,1)S(1)}, bf16[64,2,16,128]{3,2,1,0:T(8,128)(2,1)}, u32[]{:S(2)}, u32[]{:S(2)}) %collective-permute-start.4) | collective-permute-done | bytes 524320 | tf_op jit(solution)/shard_map/ppermute | solution.py:297
  52.8 2.4 %collective-permute-start.19 = (bf16[64,2,16,128]{3,2,1,0:T(8,128)(2,1)S(1)}, bf16[64,2,16,128]{3,2,1,0:T(8,128)(2,1)S(1)}, u32[]{:S(2)}, u32[]{:S(2)}) collective-permute-start(bf16[64,2,16,128]{3,2,1,0:T(8,128)(2,1)S(1)} %bitcast.39), channel_id=1, source_target_pairs={{0,6},{1,7},{2,0},{3,1},{4,2},{5,3},{6,4},{7,5},{8,14},{9,15},{10,... | collective-permute-start | bytes 1572872 | tf_op jit(solution)/shard_map/ppermute | solution.py:267
  55.6 2.3 %collective-permute-start.6 = (bf16[64,2,16,128]{3,2,1,0:T(8,128)(2,1)}, bf16[64,2,16,128]{3,2,1,0:T(8,128)(2,1)}, u32[]{:S(2)}, u32[]{:S(2)}) collective-permute-start(bf16[64,2,16,128]{3,2,1,0:T(8,128)(2,1)} %collective-permute-done.4.refs_6_), channel_id=1, source_target_pairs={{0,48},{16,0},{32,16},{48,32},{64,112},{80,64},{96,80},{112,96},{1... | collective-permute-start | bytes 1572872 | tf_op jit(solution)/shard_map/ppermute | solution.py:267
  58.1 7.3 %collective-permute-done.9.refs_4_ = bf16[64,2,16,128]{3,2,1,0:T(8,128)(2,1)} collective-permute-done((bf16[64,2,16,128]{3,2,1,0:T(8,128)(2,1)S(1)}, bf16[64,2,16,128]{3,2,1,0:T(8,128)(2,1)}, u32[]{:S(2)}, u32[]{:S(2)}) %collective-permute-start.9) | collective-permute-done | bytes 524320 | tf_op jit(solution)/shard_map/ppermute | solution.py:296
  65.8 2.4 %collective-permute-start.10 = (bf16[64,2,16,128]{3,2,1,0:T(8,128)(2,1)}, bf16[64,2,16,128]{3,2,1,0:T(8,128)(2,1)S(1)}, u32[]{:S(2)}, u32[]{:S(2)}) collective-permute-start(bf16[64,2,16,128]{3,2,1,0:T(8,128)(2,1)} %collective-permute-done.9.refs_4_), channel_id=1, source_target_pairs={{0,6},{1,7},{2,0},{3,1},{4,2},{5,3},{6,4},{7,5},{8,14},{9,15},{10,... | collective-permute-start | bytes 1572872 | tf_op jit(solution)/shard_map/ppermute | solution.py:267
  71.5 2.4 %collective-permute-start.3 = (bf16[32,2,16,128]{3,2,1,0:T(8,128)(2,1)}, bf16[32,2,16,128]{3,2,1,0:T(8,128)(2,1)}, u32[]{:S(2)}, u32[]{:S(2)}) collective-permute-start(bf16[32,2,16,128]{3,2,1,0:T(8,128)(2,1)} %slice.39), channel_id=1, source_target_pairs={{0,48},{16,0},{32,16},{48,32},{64,112},{80,64},{96,80},{112,96},{1... | collective-permute-start | bytes 786440 | tf_op jit(solution)/shard_map/ppermute | solution.py:269
  74.0 2.5 %gather_fusion.2 = f32[128,32]{1,0:T(8,128)} fusion(f32[32,2048]{0,1:T(8,128)} %copy-done.8, s32[1024]{0:T(1024)S(1)} %pad_clamp_fusion), kind=kCustom, calls=%fused_computation.2 | custom fusion | bytes 33280 | tf_op jit(solution)/shard_map/jit(_take)/gather | solution.py:289
  76.5 2.6 %gather_fusion.1 = f32[256,32]{1,0:T(8,128)} fusion(f32[32,2048]{0,1:T(8,128)} %copy-done.8, s32[1024]{0:T(1024)S(1)} %pad_clamp_fusion.1), kind=kCustom, calls=%fused_computation.1 | custom fusion | bytes 66560 | tf_op jit(solution)/shard_map/jit(_take)/gather | solution.py:288
  84.3 2.6 %collective-permute-start.23 = (bf16[32,2,16,128]{3,2,1,0:T(8,128)(2,1)}, bf16[32,2,16,128]{3,2,1,0:T(8,128)(2,1)}, u32[]{:S(2)}, u32[]{:S(2)}) collective-permute-start(bf16[32,2,16,128]{3,2,1,0:T(8,128)(2,1)} %slice.45), channel_id=1, source_target_pairs={{0,6},{1,7},{2,0},{3,1},{4,2},{5,3},{6,4},{7,5},{8,14},{9,15},{10,... | collective-permute-start | bytes 786440 | tf_op jit(solution)/shard_map/ppermute | solution.py:269
  86.9 2.7 %collective-permute-start.8 = (bf16[32,2,16,128]{3,2,1,0:T(8,128)(2,1)}, bf16[32,2,16,128]{3,2,1,0:T(8,128)(2,1)}, u32[]{:S(2)}, u32[]{:S(2)}) collective-permute-start(bf16[32,2,16,128]{3,2,1,0:T(8,128)(2,1)} %slice.41), channel_id=1, source_target_pairs={{0,48},{16,0},{32,16},{48,32},{64,112},{80,64},{96,80},{112,96},{1... | collective-permute-start | bytes 786440 | tf_op jit(solution)/shard_map/ppermute | solution.py:269
  89.7 3.6 %collective-permute-start.26 = (bf16[64,2,16,128]{3,2,1,0:T(8,128)(2,1)S(1)}, bf16[64,2,16,128]{3,2,1,0:T(8,128)(2,1)}, u32[]{:S(2)}, u32[]{:S(2)}) collective-permute-start(bf16[64,2,16,128]{3,2,1,0:T(8,128)(2,1)S(1)} %bitcast.40), channel_id=1, source_target_pairs={{0,1},{1,0},{2,3},{3,2},{4,5},{5,4},{6,7},{7,6},{8,9},{9,8},{10,11... | collective-permute-start | bytes 1572872 | tf_op jit(solution)/shard_map/ppermute | solution.py:303
  94.2 3.6 %collective-permute-start.24 = (bf16[32,2,16,128]{3,2,1,0:T(8,128)(2,1)S(1)}, bf16[32,2,16,128]{3,2,1,0:T(8,128)(2,1)S(1)}, u32[]{:S(2)}, u32[]{:S(2)}) collective-permute-start(bf16[32,2,16,128]{3,2,1,0:T(8,128)(2,1)S(1)} %collective-permute-done.22.refs_6_), channel_id=1, source_target_pairs={{0,1},{1,0},{2,3},{3,2},{4,5},{5,4},{6,7},{7,6},{8,9},{9,8},{10,11... | collective-permute-start | bytes 786440 | tf_op jit(solution)/shard_map/ppermute | solution.py:303
  98.8 4.0 %shard_map.57.refs_1_ = bf16[64,2,128,128]{3,2,1,0:T(8,128)(2,1)S(1)} custom-call(s32[8]{0:T(128)S(1)} %stack.100.refs_0_, bf16[64,2,16,128]{3,2,1,0:T(8,128)(2,1)S(1)} %bitcast.41, bf16[64,2,16,128]{3,2,1,0:T(8,128)(2,1)S(1)} %collective-permute-done.refs_2_, bf16[64,2,16,128]{3,2,1,0:T(8,128)(2,1)S(1)} %copy-done.3, ...), custom_call_target="tpu_custom_call" | custom-call | flops 4000000000 | bytes 8388608 | tf_op jit(solution)/shard_map/pallas_call | solution.py:132
  102.9 2.0 %copy-done.7 = bf16[64,2,128,128]{3,2,1,0:T(8,128)(2,1)} copy-done((bf16[64,2,128,128]{3,2,1,0:T(8,128)(2,1)}, bf16[64,2,128,128]{3,2,1,0:T(8,128)(2,1)S(1)}, u32[]{:S(2)}) %copy-start.7) | copy-done | bytes 4194328
  104.8 2.7 %collective-permute-start.14 = (bf16[32,2,16,128]{3,2,1,0:T(8,128)(2,1)S(1)}, bf16[32,2,16,128]{3,2,1,0:T(8,128)(2,1)S(1)}, u32[]{:S(2)}, u32[]{:S(2)}) collective-permute-start(bf16[32,2,16,128]{3,2,1,0:T(8,128)(2,1)S(1)} %slice.43), channel_id=1, source_target_pairs={{0,6},{1,7},{2,0},{3,1},{4,2},{5,3},{6,4},{7,5},{8,14},{9,15},{10,... | collective-permute-start | bytes 786440 | tf_op jit(solution)/shard_map/ppermute | solution.py:269
  108.5 10.5 %shard_map.58.refs_10_ = bf16[256,128,256]{2,1,0:T(8,128)(2,1)} custom-call(s32[4]{0:T(128)S(1)} %pad_add_fusion.3.refs_0_, bf16[64,2,128,128]{3,2,1,0:T(8,128)(2,1)} %copy-done.7, f32[256,128]{1,0:T(8,128)S(1)} %fusion.refs_2_, bf16[256,512]{1,0:T(8,128)(2,1)S(1)} %copy-done.5, bf16[64,2,16,128]{3,2,1,0:T(8,128)(2,1)S(1)} %bitcast.42, ...), custom_call_target="tpu_custom_call" | custom-call | flops 15000000512 | bytes 10485760 | tf_op jit(solution)/shard_map/pallas_call | solution.py:236
  121.2 10.3 %shard_map.59.refs_8_ = bf16[256,128,256]{2,1,0:T(8,128)(2,1)} custom-call(s32[4]{0:T(128)S(1)} %pad_add_fusion.2.refs_0_, bf16[64,2,128,128]{3,2,1,0:T(8,128)(2,1)} %copy-done.7, f32[256,128]{1,0:T(8,128)S(1)} %fusion.refs_2_, bf16[256,512]{1,0:T(8,128)(2,1)S(1)} %copy-done.6, ...), custom_call_target="tpu_custom_call", output_to_operand_aliasing={{}: (10, {})} | custom-call | flops 15000000512 | bytes 10485760 | tf_op jit(solution)/shard_map/pallas_call | solution.py:236
  131.5 10.4 %shard_map.60.refs_10_ = bf16[256,128,256]{2,1,0:T(8,128)(2,1)} custom-call(s32[4]{0:T(128)S(1)} %get-tuple-element.6.refs_0_, bf16[64,2,128,128]{3,2,1,0:T(8,128)(2,1)} %copy-done.7, f32[256,128]{1,0:T(8,128)S(1)} %fusion.refs_2_, bf16[256,512]{1,0:T(8,128)(2,1)S(1)} %copy-done.6, ...), custom_call_target="tpu_custom_call", output_to_operand_aliasing={{}: (8, {})} | custom-call | flops 15000000512 | bytes 10485760 | tf_op jit(solution)/shard_map/pallas_call | solution.py:236
  141.9 10.3 %shard_map.61 = bf16[256,128,256]{2,1,0:T(8,128)(2,1)} custom-call(s32[4]{0:T(128)S(1)} %get-tuple-element.5.refs_0_, bf16[64,2,128,128]{3,2,1,0:T(8,128)(2,1)} %copy-done.7, f32[256,128]{1,0:T(8,128)S(1)} %fusion.refs_2_, bf16[256,512]{1,0:T(8,128)(2,1)S(1)} %copy-done.6, ...), custom_call_target="tpu_custom_call", output_to_operand_aliasing={{}: (10, {})} | custom-call | flops 15000000512 | bytes 10485760 | tf_op jit(solution)/shard_map/pallas_call | solution.py:236
  (88 shorter events, 23.0 us)
Async XLA Ops:
  5.1 30.6 %all-to-all-start = ((bf16[128,16,150]{2,1,0:T(8,128)(2,1)}), bf16[128,16,150]{2,1,0:T(8,128)(2,1)S(1)}, u32[]{:S(2)}, u32[]{:S(2)}) async-start(bf16[128,16,150]{2,1,0:T(8,128)(2,1)} %bitcast.14), calls=%async_computation | async-start | bytes 2097152 | tf_op jit(solution)/shard_map/all_to_all | solution.py:283
  40.4 12.4 %collective-permute-start.4 = (bf16[64,2,16,128]{3,2,1,0:T(8,128)(2,1)S(1)}, bf16[64,2,16,128]{3,2,1,0:T(8,128)(2,1)}, u32[]{:S(2)}, u32[]{:S(2)}) collective-permute-start(bf16[64,2,16,128]{3,2,1,0:T(8,128)(2,1)S(1)} %bitcast.34), channel_id=1, source_target_pairs={{0,64},{16,80},{32,96},{48,112},{64,0},{80,16},{96,32},{112,48},{1... | collective-permute-start | bytes 1572872 | tf_op jit(solution)/shard_map/ppermute | solution.py:297
  40.9 14.4 %collective-permute-start = (bf16[64,2,16,128]{3,2,1,0:T(8,128)(2,1)S(1)}, bf16[64,2,16,128]{3,2,1,0:T(8,128)(2,1)S(1)}, u32[]{:S(2)}, u32[]{:S(2)}) collective-permute-start(bf16[64,2,16,128]{3,2,1,0:T(8,128)(2,1)S(1)} %bitcast.35), channel_id=1, source_target_pairs={{0,16},{16,32},{32,48},{48,0},{64,80},{80,96},{96,112},{112,64},{1... | collective-permute-start | bytes 1572872 | tf_op jit(solution)/shard_map/ppermute | solution.py:266
  40.9 14.7 %collective-permute-start.1 = (bf16[64,2,16,128]{3,2,1,0:T(8,128)(2,1)S(1)}, bf16[64,2,16,128]{3,2,1,0:T(8,128)(2,1)S(1)}, u32[]{:S(2)}, u32[]{:S(2)}) collective-permute-start(bf16[64,2,16,128]{3,2,1,0:T(8,128)(2,1)S(1)} %bitcast.36), channel_id=1, source_target_pairs={{0,48},{16,0},{32,16},{48,32},{64,112},{80,64},{96,80},{112,96},{1... | collective-permute-start | bytes 1572872 | tf_op jit(solution)/shard_map/ppermute | solution.py:267
  43.6 21.9 %collective-permute-start.9 = (bf16[64,2,16,128]{3,2,1,0:T(8,128)(2,1)S(1)}, bf16[64,2,16,128]{3,2,1,0:T(8,128)(2,1)}, u32[]{:S(2)}, u32[]{:S(2)}) collective-permute-start(bf16[64,2,16,128]{3,2,1,0:T(8,128)(2,1)S(1)} %bitcast.37), channel_id=1, source_target_pairs={{0,8},{1,9},{2,10},{3,11},{4,12},{5,13},{6,14},{7,15},{8,0},{9,1},... | collective-permute-start | bytes 1572872 | tf_op jit(solution)/shard_map/ppermute | solution.py:296
  45.2 20.5 %collective-permute-start.21 = (bf16[64,2,16,128]{3,2,1,0:T(8,128)(2,1)S(1)}, bf16[64,2,16,128]{3,2,1,0:T(8,128)(2,1)S(1)}, u32[]{:S(2)}, u32[]{:S(2)}) collective-permute-start(bf16[64,2,16,128]{3,2,1,0:T(8,128)(2,1)S(1)} %bitcast.38), channel_id=1, source_target_pairs={{0,2},{1,3},{2,4},{3,5},{4,6},{5,7},{6,0},{7,1},{8,10},{9,11},{10,... | collective-permute-start | bytes 1572872 | tf_op jit(solution)/shard_map/ppermute | solution.py:266
  52.8 18.5 %collective-permute-start.19 = (bf16[64,2,16,128]{3,2,1,0:T(8,128)(2,1)S(1)}, bf16[64,2,16,128]{3,2,1,0:T(8,128)(2,1)S(1)}, u32[]{:S(2)}, u32[]{:S(2)}) collective-permute-start(bf16[64,2,16,128]{3,2,1,0:T(8,128)(2,1)S(1)} %bitcast.39), channel_id=1, source_target_pairs={{0,6},{1,7},{2,0},{3,1},{4,2},{5,3},{6,4},{7,5},{8,14},{9,15},{10,... | collective-permute-start | bytes 1572872 | tf_op jit(solution)/shard_map/ppermute | solution.py:267
  55.3 16.3 %collective-permute-start.5 = (bf16[64,2,16,128]{3,2,1,0:T(8,128)(2,1)}, bf16[64,2,16,128]{3,2,1,0:T(8,128)(2,1)}, u32[]{:S(2)}, u32[]{:S(2)}) collective-permute-start(bf16[64,2,16,128]{3,2,1,0:T(8,128)(2,1)} %collective-permute-done.4.refs_6_), channel_id=1, source_target_pairs={{0,16},{16,32},{32,48},{48,0},{64,80},{80,96},{96,112},{112,64},{1... | collective-permute-start | bytes 1572872 | tf_op jit(solution)/shard_map/ppermute | solution.py:266
  55.6 18.3 %collective-permute-start.6 = (bf16[64,2,16,128]{3,2,1,0:T(8,128)(2,1)}, bf16[64,2,16,128]{3,2,1,0:T(8,128)(2,1)}, u32[]{:S(2)}, u32[]{:S(2)}) collective-permute-start(bf16[64,2,16,128]{3,2,1,0:T(8,128)(2,1)} %collective-permute-done.4.refs_6_), channel_id=1, source_target_pairs={{0,48},{16,0},{32,16},{48,32},{64,112},{80,64},{96,80},{112,96},{1... | collective-permute-start | bytes 1572872 | tf_op jit(solution)/shard_map/ppermute | solution.py:267
  65.5 24.2 %collective-permute-start.12 = (bf16[64,2,16,128]{3,2,1,0:T(8,128)(2,1)}, bf16[64,2,16,128]{3,2,1,0:T(8,128)(2,1)S(1)}, u32[]{:S(2)}, u32[]{:S(2)}) collective-permute-start(bf16[64,2,16,128]{3,2,1,0:T(8,128)(2,1)} %collective-permute-done.9.refs_4_), channel_id=1, source_target_pairs={{0,2},{1,3},{2,4},{3,5},{4,6},{5,7},{6,0},{7,1},{8,10},{9,11},{10,... | collective-permute-start | bytes 1572872 | tf_op jit(solution)/shard_map/ppermute | solution.py:266
  65.8 27.5 %collective-permute-start.10 = (bf16[64,2,16,128]{3,2,1,0:T(8,128)(2,1)}, bf16[64,2,16,128]{3,2,1,0:T(8,128)(2,1)S(1)}, u32[]{:S(2)}, u32[]{:S(2)}) collective-permute-start(bf16[64,2,16,128]{3,2,1,0:T(8,128)(2,1)} %collective-permute-done.9.refs_4_), channel_id=1, source_target_pairs={{0,6},{1,7},{2,0},{3,1},{4,2},{5,3},{6,4},{7,5},{8,14},{9,15},{10,... | collective-permute-start | bytes 1572872 | tf_op jit(solution)/shard_map/ppermute | solution.py:267
  71.3 13.0 %collective-permute-start.2 = (bf16[32,2,16,128]{3,2,1,0:T(8,128)(2,1)}, bf16[32,2,16,128]{3,2,1,0:T(8,128)(2,1)}, u32[]{:S(2)}, u32[]{:S(2)}) collective-permute-start(bf16[32,2,16,128]{3,2,1,0:T(8,128)(2,1)} %slice.38), channel_id=1, source_target_pairs={{0,16},{16,32},{32,48},{48,0},{64,80},{80,96},{96,112},{112,64},{1... | collective-permute-start | bytes 786440 | tf_op jit(solution)/shard_map/ppermute | solution.py:269
  71.5 15.4 %collective-permute-start.3 = (bf16[32,2,16,128]{3,2,1,0:T(8,128)(2,1)}, bf16[32,2,16,128]{3,2,1,0:T(8,128)(2,1)}, u32[]{:S(2)}, u32[]{:S(2)}) collective-permute-start(bf16[32,2,16,128]{3,2,1,0:T(8,128)(2,1)} %slice.39), channel_id=1, source_target_pairs={{0,48},{16,0},{32,16},{48,32},{64,112},{80,64},{96,80},{112,96},{1... | collective-permute-start | bytes 786440 | tf_op jit(solution)/shard_map/ppermute | solution.py:269
  74.0 13.0 %collective-permute-start.22 = (bf16[32,2,16,128]{3,2,1,0:T(8,128)(2,1)}, bf16[32,2,16,128]{3,2,1,0:T(8,128)(2,1)S(1)}, u32[]{:S(2)}, u32[]{:S(2)}) collective-permute-start(bf16[32,2,16,128]{3,2,1,0:T(8,128)(2,1)} %slice.44), channel_id=1, source_target_pairs={{0,2},{1,3},{2,4},{3,5},{4,6},{5,7},{6,0},{7,1},{8,10},{9,11},{10,... | collective-permute-start | bytes 786440 | tf_op jit(solution)/shard_map/ppermute | solution.py:269
  89.7 15.2 %collective-permute-start.26 = (bf16[64,2,16,128]{3,2,1,0:T(8,128)(2,1)S(1)}, bf16[64,2,16,128]{3,2,1,0:T(8,128)(2,1)}, u32[]{:S(2)}, u32[]{:S(2)}) collective-permute-start(bf16[64,2,16,128]{3,2,1,0:T(8,128)(2,1)S(1)} %bitcast.40), channel_id=1, source_target_pairs={{0,1},{1,0},{2,3},{3,2},{4,5},{5,4},{6,7},{7,6},{8,9},{9,8},{10,11... | collective-permute-start | bytes 1572872 | tf_op jit(solution)/shard_map/ppermute | solution.py:303
  93.7 26.5 %collective-permute-start.20 = (bf16[64,2,16,128]{3,2,1,0:T(8,128)(2,1)S(1)}, bf16[64,2,16,128]{3,2,1,0:T(8,128)(2,1)S(1)}, u32[]{:S(2)}, u32[]{:S(2)}) collective-permute-start(bf16[64,2,16,128]{3,2,1,0:T(8,128)(2,1)S(1)} %collective-permute-done.19.refs_4_), channel_id=1, source_target_pairs={{0,1},{1,0},{2,3},{3,2},{4,5},{5,4},{6,7},{7,6},{8,9},{9,8},{10,11... | collective-permute-start | bytes 1572872 | tf_op jit(solution)/shard_map/ppermute | solution.py:303
  94.2 24.8 %collective-permute-start.24 = (bf16[32,2,16,128]{3,2,1,0:T(8,128)(2,1)S(1)}, bf16[32,2,16,128]{3,2,1,0:T(8,128)(2,1)S(1)}, u32[]{:S(2)}, u32[]{:S(2)}) collective-permute-start(bf16[32,2,16,128]{3,2,1,0:T(8,128)(2,1)S(1)} %collective-permute-done.22.refs_6_), channel_id=1, source_target_pairs={{0,1},{1,0},{2,3},{3,2},{4,5},{5,4},{6,7},{7,6},{8,9},{9,8},{10,11... | collective-permute-start | bytes 786440 | tf_op jit(solution)/shard_map/ppermute | solution.py:303
  97.8 22.4 %collective-permute-start.25 = (bf16[32,2,16,128]{3,2,1,0:T(8,128)(2,1)}, bf16[32,2,16,128]{3,2,1,0:T(8,128)(2,1)S(1)}, u32[]{:S(2)}, u32[]{:S(2)}) collective-permute-start(bf16[32,2,16,128]{3,2,1,0:T(8,128)(2,1)} %collective-permute-done.23.refs_7_), channel_id=1, source_target_pairs={{0,1},{1,0},{2,3},{3,2},{4,5},{5,4},{6,7},{7,6},{8,9},{9,8},{10,11... | collective-permute-start | bytes 786440 | tf_op jit(solution)/shard_map/ppermute | solution.py:303
  104.8 15.8 %collective-permute-start.13 = (bf16[32,2,16,128]{3,2,1,0:T(8,128)(2,1)S(1)}, bf16[32,2,16,128]{3,2,1,0:T(8,128)(2,1)S(1)}, u32[]{:S(2)}, u32[]{:S(2)}) collective-permute-start(bf16[32,2,16,128]{3,2,1,0:T(8,128)(2,1)S(1)} %slice.42), channel_id=1, source_target_pairs={{0,2},{1,3},{2,4},{3,5},{4,6},{5,7},{6,0},{7,1},{8,10},{9,11},{10,... | collective-permute-start | bytes 786440 | tf_op jit(solution)/shard_map/ppermute | solution.py:269
  104.8 15.9 %collective-permute-start.14 = (bf16[32,2,16,128]{3,2,1,0:T(8,128)(2,1)S(1)}, bf16[32,2,16,128]{3,2,1,0:T(8,128)(2,1)S(1)}, u32[]{:S(2)}, u32[]{:S(2)}) collective-permute-start(bf16[32,2,16,128]{3,2,1,0:T(8,128)(2,1)S(1)} %slice.43), channel_id=1, source_target_pairs={{0,6},{1,7},{2,0},{3,1},{4,2},{5,3},{6,4},{7,5},{8,14},{9,15},{10,... | collective-permute-start | bytes 786440 | tf_op jit(solution)/shard_map/ppermute | solution.py:269
  119.0 12.5 %collective-permute-start.17 = (bf16[64,2,16,128]{3,2,1,0:T(8,128)(2,1)}, bf16[64,2,16,128]{3,2,1,0:T(8,128)(2,1)S(1)}, u32[]{:S(2)}, u32[]{:S(2)}) collective-permute-start(bf16[64,2,16,128]{3,2,1,0:T(8,128)(2,1)} %collective-permute-done.9.refs_4_), channel_id=1, source_target_pairs={{0,1},{1,0},{2,3},{3,2},{4,5},{5,4},{6,7},{7,6},{8,9},{9,8},{10,11... | collective-permute-start | bytes 1572872 | tf_op jit(solution)/shard_map/ppermute | solution.py:303
  120.3 21.7 %collective-permute-start.11 = (bf16[64,2,16,128]{3,2,1,0:T(8,128)(2,1)S(1)}, bf16[64,2,16,128]{3,2,1,0:T(8,128)(2,1)S(1)}, u32[]{:S(2)}, u32[]{:S(2)}) collective-permute-start(bf16[64,2,16,128]{3,2,1,0:T(8,128)(2,1)S(1)} %collective-permute-done.10.refs_4_), channel_id=1, source_target_pairs={{0,1},{1,0},{2,3},{3,2},{4,5},{5,4},{6,7},{7,6},{8,9},{9,8},{10,11... | collective-permute-start | bytes 1572872 | tf_op jit(solution)/shard_map/ppermute | solution.py:303
  120.7 21.2 %collective-permute-start.15 = (bf16[32,2,16,128]{3,2,1,0:T(8,128)(2,1)S(1)}, bf16[32,2,16,128]{3,2,1,0:T(8,128)(2,1)S(1)}, u32[]{:S(2)}, u32[]{:S(2)}) collective-permute-start(bf16[32,2,16,128]{3,2,1,0:T(8,128)(2,1)S(1)} %collective-permute-done.13.refs_6_), channel_id=1, source_target_pairs={{0,1},{1,0},{2,3},{3,2},{4,5},{5,4},{6,7},{7,6},{8,9},{9,8},{10,11... | collective-permute-start | bytes 786440 | tf_op jit(solution)/shard_map/ppermute | solution.py:303
  120.8 21.1 %collective-permute-start.16 = (bf16[32,2,16,128]{3,2,1,0:T(8,128)(2,1)S(1)}, bf16[32,2,16,128]{3,2,1,0:T(8,128)(2,1)S(1)}, u32[]{:S(2)}, u32[]{:S(2)}) collective-permute-start(bf16[32,2,16,128]{3,2,1,0:T(8,128)(2,1)S(1)} %collective-permute-done.14.refs_7_), channel_id=1, source_target_pairs={{0,1},{1,0},{2,3},{3,2},{4,5},{5,4},{6,7},{7,6},{8,9},{9,8},{10,11... | collective-permute-start | bytes 786440 | tf_op jit(solution)/shard_map/ppermute | solution.py:303
  (14 other events, 90.8 us)
